TPU v7x, 128 devices: a whole 4x4x4 slice. The times are simulated.
128 devices in a mesh: dp: 8 (over z, core), tensor: 16 (over y, x).
Axes of the slice: x: 4, y: 4, z: 4, core: 2. Of those that a mesh axis runs over, the one named last changes fastest.
Arguments:
- h_in: bfloat16 [1024, 8192], P('dp'), may hold values from -6 to 6
- dout: bfloat16 [1024, 8192], P('dp'), may hold values from -6 to 6
- w_gate: bfloat16 [28672, 512], P('tensor'), may hold values from -0.25 to 0.25
- w_up: bfloat16 [28672, 512], P('tensor'), may hold values from -0.25 to 0.25
- w_down: bfloat16 [28672, 512], P('tensor'), may hold values from -0.125 to 0.125
- in_layout: int32 [224, 4], P('tensor'), may hold values from 0 to 63, all different within a row
- out_layout: int32 [224, 4], P('tensor'), may hold values from 0 to 63, all different within a row
Outputs:
- out: bfloat16 [1024, 8192], P('dp', 'tensor')
- dh: bfloat16 [1024, 8192], P('dp', 'tensor')
- grad_gate: float32 [224, 65536], P('tensor', 'dp')
- grad_up: float32 [224, 65536], P('tensor', 'dp')
- grad_down: float32 [224, 65536], P('tensor', 'dp')
Inputs may be any that keep to these rules, and one draw needn't show every extreme that they name: `in_layout`: each block row names 4 different blocks; every block is named by some block row. `out_layout`: each block row names 4 different blocks; every block is named by some block row.
All inputs are finite; a program needn't handle non-finite values.
Results may differ from a plain program's by a relative error of at most 0.018.
Values may be sent and summed in bfloat16 or wider, within the bound.
No kernel may reach another device: no remote copies, remote signals or barrier semaphores. Data moves between devices by JAX's collectives and lax.ppermute only.
A program may use at most 128 MiB of HBM per device.

v0:
```python
import jax
import jax.numpy as jnp
from jax import lax
from jax.sharding import PartitionSpec as P

D = 8192
BLK = 128
KB = 4


def block_sum(values, layout_flat, tokens, nblocks):
    empty = jnp.zeros((tokens, nblocks, BLK), jnp.float32)
    return empty.at[:, layout_flat].add(values).reshape(tokens, nblocks * BLK)


def shards(h_in, dout, w_gate, w_up, w_down, in_layout, out_layout):
    tokens = h_in.shape[0]
    rows_grp = in_layout.shape[0]
    nblocks = D // BLK
    lin_flat = in_layout.reshape(-1)
    lout_flat = out_layout.reshape(-1)
    wg = w_gate.reshape(rows_grp, BLK, KB * BLK)
    wu = w_up.reshape(rows_grp, BLK, KB * BLK)
    wd = w_down.reshape(rows_grp, BLK, KB * BLK)
    hx = jnp.take(h_in.reshape(tokens, nblocks, BLK), lin_flat, axis=1).reshape(
        tokens, rows_grp, KB * BLK
    )
    gate = jnp.einsum("trm,rim->tri", hx, wg, preferred_element_type=jnp.float32)
    up = jnp.einsum("trm,rim->tri", hx, wu, preferred_element_type=jnp.float32)
    sig = jax.nn.sigmoid(gate)
    act = gate * sig
    hidden = (act * up).astype(jnp.bfloat16)
    contrib = jnp.einsum("tri,rim->trm", hidden, wd, preferred_element_type=jnp.float32)
    partial_out = block_sum(contrib.reshape(tokens, rows_grp * KB, BLK), lout_flat, tokens, nblocks)
    partial_out = partial_out.astype(jnp.bfloat16).astype(jnp.float32)
    out = lax.psum_scatter(
        partial_out.astype(jnp.bfloat16), "tensor", scatter_dimension=1, tiled=True
    )
    dob = jnp.take(dout.reshape(tokens, nblocks, BLK), lout_flat, axis=1).reshape(
        tokens, rows_grp, KB * BLK
    )
    dhid = jnp.einsum("trm,rim->tri", dob, wd, preferred_element_type=jnp.float32)
    g_down = jnp.einsum("tri,trm->rim", hidden, dob, preferred_element_type=jnp.float32).reshape(
        rows_grp, -1
    )
    dgate = (dhid * up * sig * (1.0 + gate * (1.0 - sig))).astype(jnp.bfloat16)
    dup = (dhid * act).astype(jnp.bfloat16)
    g_gate = jnp.einsum("tri,trm->rim", dgate, hx, preferred_element_type=jnp.float32).reshape(
        rows_grp, -1
    )
    g_up = jnp.einsum("tri,trm->rim", dup, hx, preferred_element_type=jnp.float32).reshape(
        rows_grp, -1
    )
    summed_gate, summed_up, summed_down = (
        lax.psum(g_gate.astype(jnp.bfloat16), "dp").astype(jnp.float32),
        lax.psum(g_up.astype(jnp.bfloat16), "dp").astype(jnp.float32),
        lax.psum(g_down.astype(jnp.bfloat16), "dp").astype(jnp.float32),
    )
    share = summed_gate.shape[1] // lax.axis_size("dp")
    offset = lax.axis_index("dp") * share
    gate_part = lax.dynamic_slice_in_dim(summed_gate, offset, share, 1)
    up_part = lax.dynamic_slice_in_dim(summed_up, offset, share, 1)
    down_part = lax.dynamic_slice_in_dim(summed_down, offset, share, 1)
    dhx = jnp.einsum("tri,rim->trm", dgate, wg, preferred_element_type=jnp.float32)
    dhx = dhx + jnp.einsum("tri,rim->trm", dup, wu, preferred_element_type=jnp.float32)
    partial_dh = block_sum(dhx.reshape(tokens, rows_grp * KB, BLK), lin_flat, tokens, nblocks)
    partial_dh = partial_dh.astype(jnp.bfloat16).astype(jnp.float32)
    dh = lax.psum_scatter(
        partial_dh.astype(jnp.bfloat16), "tensor", scatter_dimension=1, tiled=True
    )
    return (out, dh, gate_part, up_part, down_part)


def solution(mesh):
    placed = (
        P("dp", None),
        P("dp", None),
        P("tensor", None),
        P("tensor", None),
        P("tensor", None),
        P("tensor", None),
        P("tensor", None),
    )
    return jax.shard_map(
        shards,
        mesh=mesh,
        in_specs=placed,
        out_specs=(
            P("dp", "tensor"),
            P("dp", "tensor"),
            P("tensor", "dp"),
            P("tensor", "dp"),
            P("tensor", "dp"),
        ),
        check_vma=False,
    )
```

profile of v0, /device:TPU:0, one launch (start us, length us, event | category | flops | bytes accessed | tf_op | source)
XLA Modules:
  0.0 268.9 jit_solution(1614522637076494654)
XLA Ops:
  8.0 0.0 copy-start
  8.0 0.0 all-reduce.3.cloned.1.call-start
  8.1 0.9 copy.43
  9.0 0.1 reshape.120
  9.0 0.8 copy.42
  9.8 0.1 reshape.128
  9.9 4.1 %copy.44 = bf16[128,8192]{0,1:T(8,128)(2,1)} copy(bf16[128,8192]{1,0:T(8,128)(2,1)} %param.9) | data formatting | bytes 4194304 | tf_op args[0]
  14.0 4.1 %copy.45 = bf16[128,64,128]{2,0,1:T(8,128)(2,1)} copy(bf16[128,64,128]{0,2,1:T(8,128)(2,1)} %bitcast.76) | data formatting | bytes 4194304 | tf_op jit(solution)/shard_map/reshape | solution.py:25
  18.1 3.6 %gather_fusion = bf16[56,128,128]{2,1,0:T(8,128)(2,1)} fusion(bf16[128,64,128]{2,0,1:T(8,128)(2,1)} %copy.45, s32[1024]{0:T(1024)S(1)} %pad_clamp_fusion.1), kind=kCustom, calls=%fused_computation.clone | custom fusion | bytes 3670240 | tf_op jit(solution)/shard_map/jit(_take)/gather | solution.py:25
  21.7 3.0 %select_bitcast_fusion.1 = bf16[128,56,128]{2,0,1:T(8,128)(2,1)} fusion(bf16[56,128,128]{2,1,0:T(8,128)(2,1)} %gather_fusion, pred[56]{0:T(512)(128)(4,1)S(1)} %get-tuple-element.25), kind=kLoop, calls=%fused_computation.7 | loop fusion | flops 917504 | bytes 3670072 | tf_op jit(solution)/shard_map/jit(_take)/select_n | solution.py:25
  24.7 3.9 %copy.46 = bf16[128,56,128]{0,2,1:T(8,128)(2,1)} copy(bf16[128,56,128]{2,0,1:T(8,128)(2,1)} %select_bitcast_fusion.1) | data formatting | bytes 3670016 | tf_op jit(solution)/shard_map/jit(_take)/select_n | solution.py:25
  28.6 3.9 %convolution_bitcast_fusion.2 = f32[128,14,128]{2,0,1:T(8,128)} fusion(bf16[128,14,512]{0,2,1:T(8,128)(2,1)} %bitcast.62, bf16[14,128,512]{2,1,0:T(8,128)(2,1)} %bitcast.78), kind=kOutput, calls=%fused_computation.12 | convolution fusion | flops 234881024 | bytes 4587520 | tf_op jit(solution)/shard_map/trm,rim->tri/dot_general | solution.py:29
  32.5 0.0 copy-done.1
  32.5 0.0 copy-done.4
  32.5 1.7 convolution_bitcast_fusion.3
  34.2 4.1 %copy.54 = bf16[128,8192]{0,1:T(8,128)(2,1)} copy(bf16[128,8192]{1,0:T(8,128)(2,1)} %param.10) | data formatting | bytes 4194304 | tf_op args[1]
  38.3 4.1 %copy.55 = bf16[128,64,128]{2,0,1:T(8,128)(2,1)} copy(bf16[128,64,128]{0,2,1:T(8,128)(2,1)} %bitcast.77) | data formatting | bytes 4194304 | tf_op jit(solution)/shard_map/reshape | solution.py:39
  42.4 3.6 %gather_fusion.1 = bf16[56,128,128]{2,1,0:T(8,128)(2,1)} fusion(bf16[128,64,128]{2,0,1:T(8,128)(2,1)} %copy.55, s32[1024]{0:T(1024)S(1)} %pad_clamp_fusion), kind=kCustom, calls=%fused_computation.1.clone | custom fusion | bytes 3670240 | tf_op jit(solution)/shard_map/jit(_take)/gather | solution.py:39
  46.0 3.0 %select_bitcast_fusion = bf16[128,56,128]{2,0,1:T(8,128)(2,1)} fusion(bf16[56,128,128]{2,1,0:T(8,128)(2,1)} %gather_fusion.1, pred[56]{0:T(512)(128)(4,1)S(1)} %get-tuple-element.24), kind=kLoop, calls=%fused_computation.6 | loop fusion | flops 917504 | bytes 3670072 | tf_op jit(solution)/shard_map/jit(_take)/select_n | solution.py:39
  49.0 3.9 %copy.56 = bf16[128,56,128]{0,2,1:T(8,128)(2,1)} copy(bf16[128,56,128]{2,0,1:T(8,128)(2,1)} %select_bitcast_fusion) | data formatting | bytes 3670016 | tf_op jit(solution)/shard_map/jit(_take)/select_n | solution.py:39
  52.9 3.1 %multiply_convert_fusion = (bf16[128,14,128]{2,0,1:T(8,128)(2,1)S(1)}, bf16[128,14,128]{2,0,1:T(8,128)(2,1)S(1)}, bf16[128,14,128]{2,0,1:T(8,128)(2,1)S(1)}) fusion(f32[128,14,128]{2,0,1:T(8,128)} %convolution_bitcast_fusion.3, f32[128,14,128]{2,0,1:T(8,128)} %convolution_bitcast_fusion.2, bf16[128,14,512]{0,2,1:T(8,128)(2,1)} %bitcast.82, ...), kind=kOutput, calls=%fused_computation.14 | convolution fusion | flops 238321664 | bytes 6881280 | tf_op jit(solution)/shard_map/trm,rim->tri/dot_general | solution.py:42
  55.9 0.7 convolution_convert_fusion.2
  56.6 0.2 pad.2
  56.9 2.6 copy.78
  59.4 0.7 convolution_convert_fusion.1
  60.1 0.2 pad.3
  60.4 0.0 copy-start.5
  60.4 2.5 copy.79
  62.9 0.0 copy-done.5
  62.9 0.7 convolution_convert_fusion
  63.6 0.2 pad.4
  63.8 2.5 copy.80
  66.3 0.0 all-reduce.3.cloned.1.call-update
  66.3 0.2 reduce-scatter.5.cloned.1.call-start
  66.5 0.1 reshape.118
  66.6 0.1 reshape.126
  66.7 0.0 copy-start.3
  66.7 2.3 fusion.3
  69.0 0.0 copy-done.3
  69.0 2.5 add_bitcast_fusion
  71.5 5.1 %copy.58 = f32[128,14,512]{0,2,1:T(8,128)} copy(f32[128,14,512]{2,0,1:T(8,128)} %add_bitcast_fusion) | data formatting | bytes 7340032 | tf_op jit(solution)/shard_map/add | solution.py:65
  76.6 5.5 %copy.59 = f32[56,128,128]{2,1,0:T(8,128)} copy(f32[56,128,128]{1,2,0:T(8,128)} %bitcast.66) | data formatting | bytes 7340032 | tf_op jit(solution)/shard_map/reshape | solution.py:66
  82.0 2.5 broadcast.43.clone.1
  84.5 13.5 %scatter_fusion.1 = f32[128,64,128]{2,0,1:T(8,128)} fusion(f32[128,64,128]{2,0,1:T(8,128)} %broadcast.43.clone.1, s32[56]{0:T(128)S(1)} %get-tuple-element.27, f32[56,128,128]{2,1,0:T(8,128)} %copy.59), kind=kCustom, calls=%fused_computation.3 | custom fusion | flops 917504 | bytes 11010272 | tf_op jit(solution)/shard_map/scatter-add | solution.py:13
  98.0 4.0 %convert_element_type.57 = bf16[128,64,128]{2,0,1:T(8,128)(2,1)} convert(f32[128,64,128]{2,0,1:T(8,128)} %scatter_fusion.1) | non-fusion elementwise | flops 1048576 | bytes 6291456 | tf_op jit(solution)/shard_map/convert_element_type | solution.py:67
  102.0 4.1 %copy.60 = bf16[128,64,128]{0,2,1:T(8,128)(2,1)} copy(bf16[128,64,128]{2,0,1:T(8,128)(2,1)} %convert_element_type.57) | data formatting | bytes 4194304 | tf_op jit(solution)/shard_map/convert_element_type | solution.py:67
  106.1 0.0 reduce-scatter.5.cloned.1.call-update
  106.1 0.0 reduce-scatter.3.cloned.1.call-start
  106.2 2.5 convolution_bitcast_fusion
  108.6 5.1 %copy.49 = f32[128,14,512]{0,2,1:T(8,128)} copy(f32[128,14,512]{2,0,1:T(8,128)} %convolution_bitcast_fusion) | data formatting | bytes 7340032 | tf_op jit(solution)/shard_map/tri,rim->trm/transpose | solution.py:33
  113.7 5.2 %copy.50 = f32[56,128,128]{2,1,0:T(8,128)} copy(f32[56,128,128]{1,2,0:T(8,128)} %bitcast.67) | data formatting | bytes 7340032 | tf_op jit(solution)/shard_map/reshape | solution.py:34
  119.0 2.5 broadcast.43.clone
  121.4 13.6 %scatter_fusion = f32[128,64,128]{2,0,1:T(8,128)} fusion(f32[128,64,128]{2,0,1:T(8,128)} %broadcast.43.clone, s32[56]{0:T(128)S(1)} %get-tuple-element.26, f32[56,128,128]{2,1,0:T(8,128)} %copy.50), kind=kCustom, calls=%fused_computation.2 | custom fusion | flops 917504 | bytes 11010272 | tf_op jit(solution)/shard_map/scatter-add | solution.py:13
  135.0 4.0 %convert_element_type.53 = bf16[128,64,128]{2,0,1:T(8,128)(2,1)} convert(f32[128,64,128]{2,0,1:T(8,128)} %scatter_fusion) | non-fusion elementwise | flops 1048576 | bytes 6291456 | tf_op jit(solution)/shard_map/convert_element_type | solution.py:35
  139.0 4.2 %copy.51 = bf16[128,64,128]{0,2,1:T(8,128)(2,1)} copy(bf16[128,64,128]{2,0,1:T(8,128)(2,1)} %convert_element_type.53) | data formatting | bytes 4194304 | tf_op jit(solution)/shard_map/convert_element_type | solution.py:35
  143.1 0.0 reduce-scatter.3.cloned.1.call-update
  143.2 10.7 %all-reduce.3.cloned.1.call-done = (bf16[14,65536]{1,0:T(8,128)(2,1)}, bf16[14,65536]{1,0:T(8,128)(2,1)}, bf16[14,65536]{1,0:T(8,128)(2,1)}) async-done(((bf16[14,65536]{1,0:T(8,128)(2,1)}, bf16[14,65536]{1,0:T(8,128)(2,1)}, bf16[14,65536]{1,0:T(8,128)(2,1)}), (bf16[14,65536]{1,0:T(8,128)(2,1)}, bf16[14,65536]{1,0:T(8,128)(2,1)}, bf16[14,65536]{1,0:T(8,128)(2,1)})) %all-reduce.3.cloned.1.call-update) | async-done | bytes 5505040 | tf_op jit(solution)/shard_map/psum | solution.py:55
  153.9 1.8 dynamic-slice_convert_fusion
  155.7 1.8 dynamic-slice_convert_fusion.1
  157.4 1.8 dynamic-slice_convert_fusion.2
  159.2 23.3 %reduce-scatter.5.cloned.1.call-done = bf16[128,512]{0,1:T(8,128)(2,1)} async-done(((bf16[128,8192]{0,1:T(8,128)(2,1)}), bf16[128,512]{0,1:T(8,128)(2,1)}) %reduce-scatter.5.cloned.1.call-update) | async-done | bytes 131088 | tf_op jit(solution)/shard_map/reduce_scatter | solution.py:68
  182.6 1.7 copy.68
  184.2 75.6 %reduce-scatter.3.cloned.1.call-done = bf16[128,512]{0,1:T(8,128)(2,1)} async-done(((bf16[128,8192]{0,1:T(8,128)(2,1)}), bf16[128,512]{0,1:T(8,128)(2,1)}) %reduce-scatter.3.cloned.1.call-update) | async-done | bytes 131088 | tf_op jit(solution)/shard_map/reduce_scatter | solution.py:36
  259.8 1.7 copy.67
  (10 shorter events, 0.0 us)
Async XLA Ops:
  8.0 44.9 %copy-start = (bf16[1792,512]{1,0:T(8,128)(2,1)S(1)}, bf16[1792,512]{1,0:T(8,128)(2,1)}, u32[]{:S(2)}) copy-start(bf16[1792,512]{1,0:T(8,128)(2,1)} %param.13) | copy-start | bytes 5505028
  8.0 145.9 %all-reduce.3.cloned.1.call-start = ((), (), s32[]{:S(2)}) async-start(), calls=%async_computation.4 | async-start | bytes 12582912 | tf_op jit(solution)/shard_map/psum | solution.py:55
  28.6 3.9 %copy-start.1 = (bf16[128,56,128]{0,2,1:T(8,128)(2,1)S(1)}, bf16[128,56,128]{0,2,1:T(8,128)(2,1)}, u32[]{:S(2)}) copy-start(bf16[128,56,128]{0,2,1:T(8,128)(2,1)} %copy.46) | copy-start | bytes 5505028
  28.6 3.9 %copy-start.4 = (bf16[1792,512]{1,0:T(8,128)(2,1)S(1)}, bf16[1792,512]{1,0:T(8,128)(2,1)}, u32[]{:S(2)}) copy-start(bf16[1792,512]{1,0:T(8,128)(2,1)} %param.11) | copy-start | bytes 5505028
  52.8 3.1 %copy-start.2 = (bf16[128,56,128]{0,2,1:T(8,128)(2,1)S(1)}, bf16[128,56,128]{0,2,1:T(8,128)(2,1)}, u32[]{:S(2)}) copy-start(bf16[128,56,128]{0,2,1:T(8,128)(2,1)} %copy.46) | copy-start | bytes 5505028
  60.4 2.5 copy-start.5
  66.3 116.3 %reduce-scatter.5.cloned.1.call-start = ((), (), s32[]{:S(2)}) async-start(), calls=%async_computation.3 | async-start | bytes 2228224 | tf_op jit(solution)/shard_map/reduce_scatter | solution.py:68
  66.7 2.3 copy-start.3
  106.1 153.7 %reduce-scatter.3.cloned.1.call-start = ((), (), s32[]{:S(2)}) async-start(), calls=%async_computation.2 | async-start | bytes 2228224 | tf_op jit(solution)/shard_map/reduce_scatter | solution.py:36
Sparse Core Ops, SparseCore 0:
  66.4 87.4 all-reduce.2
Sparse Core Ops, SparseCore 1:
  106.2 76.3 reduce-scatter.4
  186.0 73.7 reduce-scatter.2
where the time goes:
time: 270 us; the launch traced here: 269 us
  waiting for transfers between devices  110 us (41%)
  local copies, waits for them, and re-layouts  79 us (29%)
  other arithmetic  46.3 us (17%)
  matrix products  18 us (7%)
  between operations  15.6 us (6%)
    reduce_scatter x1, waiting for transfers between devices, shards(): lax.psum_scatter(partial_out.astype(jnp.bfloat16), 'tensor', scatter_dime...  75.6 us
    scatter-add x2, other arithmetic, block_sum(): return empty.at[:, layout_flat].add(values).reshape(tokens, nblocks * BLK)  27.1 us
    reduce_scatter x1, waiting for transfers between devices, shards(): lax.psum_scatter(partial_dh.astype(jnp.bfloat16), 'tensor', scatter_dimen...  23.3 us
    unnamed x24, local copies, waits for them, and re-layouts  21.4 us
    psum x1, waiting for transfers between devices, shards(): lax.psum(g_gate.astype(jnp.bfloat16), 'dp').astype(jnp.float32)  10.7 us
    reshape x1, local copies, waits for them, and re-layouts, shards(): dhx.reshape(tokens, rows_grp * KB, BLK)  5.46 us
  transfers between devices with their start and end apart: 3, of which 3 were waited for; matrix products, arithmetic and copies ran while one was open for 31% of the time, Pallas kernels for 0%

commit v1 on v0

--- a/solution.py
+++ b/solution.py
@@ -52,7 +52,7 @@
         rows_grp, -1
     )
     summed_gate, summed_up, summed_down = (
-        lax.psum(g_gate.astype(jnp.bfloat16), "dp").astype(jnp.float32),
+        jnp.sum(lax.all_gather(g_gate.astype(jnp.bfloat16), "dp"), axis=0).astype(jnp.float32),
         lax.psum(g_up.astype(jnp.bfloat16), "dp").astype(jnp.float32),
         lax.psum(g_down.astype(jnp.bfloat16), "dp").astype(jnp.float32),
     )

time: 270 us -> 280 us (1.037)
  other arithmetic: 46.3 us -> 57.2 us
  waiting for transfers between devices: 110 us -> 105 us
    reduce_sum x0 -> x1, other arithmetic: none -> 11 us  [shards(): jnp.sum(lax.all_gather(g_gate.astype(jnp.bfloat16), 'dp'), axis=0)]
    psum x1, waiting for transfers between devices: 10.7 us -> 0.02 us  [shards(): lax.psum(g_up.astype(jnp.bfloat16), 'dp').astype(jnp.float32)]
    reduce_scatter x1, waiting for transfers between devices: 23.3 us -> 29.2 us  [shards(): lax.psum_scatter(partial_dh.astype(jnp.bfloat16), 'tensor', scatter_dimen...]
    convert_element_type x0 -> x1, local copies, waits for them, and re-layouts: none -> 3.17 us  [shards(): g_gate.astype(jnp.bfloat16)]
    unnamed x24 -> x22, local copies, waits for them, and re-layouts: 21.4 us -> 18.7 us
  transfers between devices with their start and end apart: 3 -> 4, of which waited for: 3 -> 2; matrix products, arithmetic and copies ran while one was open for 31% -> 32% of each run, Pallas kernels for 0% -> 0%
where the time goes in v1:
time: 280 us; the launch traced here: 278 us
  waiting for transfers between devices  105 us (38%)
  local copies, waits for them, and re-layouts  79.5 us (28%)
  other arithmetic  57.2 us (20%)
  matrix products  20.5 us (7%)
  between operations  15.6 us (6%)
    reduce_scatter x1, waiting for transfers between devices, shards(): lax.psum_scatter(partial_out.astype(jnp.bfloat16), 'tensor', scatter_dime...  75.5 us
    reduce_scatter x1, waiting for transfers between devices, shards(): lax.psum_scatter(partial_dh.astype(jnp.bfloat16), 'tensor', scatter_dimen...  29.2 us
    scatter-add x2, other arithmetic, block_sum(): return empty.at[:, layout_flat].add(values).reshape(tokens, nblocks * BLK)  27 us
    unnamed x22, local copies, waits for them, and re-layouts  18.7 us
    reduce_sum x1, other arithmetic, shards(): jnp.sum(lax.all_gather(g_gate.astype(jnp.bfloat16), 'dp'), axis=0)  11 us
  transfers between devices with their start and end apart: 4, of which 2 were waited for; matrix products, arithmetic and copies ran while one was open for 32% of the time, Pallas kernels for 0%

profile of v1, /device:TPU:0, one launch (start us, length us, event | category | flops | bytes accessed | tf_op | source)
XLA Modules:
  0.0 278.1 jit_solution(3761433038064757085)
XLA Ops:
  8.0 0.0 copy-start
  8.0 0.0 all-reduce.3.cloned.1.call-start
  8.1 0.9 copy.70
  9.0 0.1 reshape.130
  9.0 0.8 copy.69
  9.8 0.1 reshape.138
  9.9 4.1 %copy.71 = bf16[128,8192]{0,1:T(8,128)(2,1)} copy(bf16[128,8192]{1,0:T(8,128)(2,1)} %param.9) | data formatting | bytes 4194304 | tf_op args[0]
  14.0 4.1 %copy.72 = bf16[128,64,128]{2,0,1:T(8,128)(2,1)} copy(bf16[128,64,128]{0,2,1:T(8,128)(2,1)} %bitcast.71) | data formatting | bytes 4194304 | tf_op jit(solution)/shard_map/reshape | solution.py:25
  18.1 3.6 %gather_fusion = bf16[56,128,128]{2,1,0:T(8,128)(2,1)} fusion(bf16[128,64,128]{2,0,1:T(8,128)(2,1)} %copy.72, s32[1024]{0:T(1024)S(1)} %pad_clamp_fusion.1), kind=kCustom, calls=%fused_computation.clone | custom fusion | bytes 3670240 | tf_op jit(solution)/shard_map/jit(_take)/gather | solution.py:25
  21.7 3.0 %select_bitcast_fusion.1 = bf16[128,56,128]{2,0,1:T(8,128)(2,1)} fusion(bf16[56,128,128]{2,1,0:T(8,128)(2,1)} %gather_fusion, pred[56]{0:T(512)(128)(4,1)S(1)} %get-tuple-element.29), kind=kLoop, calls=%fused_computation.7 | loop fusion | flops 917504 | bytes 3670072 | tf_op jit(solution)/shard_map/jit(_take)/select_n | solution.py:25
  24.7 3.9 %copy.73 = bf16[128,56,128]{0,2,1:T(8,128)(2,1)} copy(bf16[128,56,128]{2,0,1:T(8,128)(2,1)} %select_bitcast_fusion.1) | data formatting | bytes 3670016 | tf_op jit(solution)/shard_map/jit(_take)/select_n | solution.py:25
  28.6 3.9 %convolution_bitcast_fusion.2 = f32[128,14,128]{2,0,1:T(8,128)} fusion(bf16[128,14,512]{0,2,1:T(8,128)(2,1)} %bitcast.59, bf16[14,128,512]{2,1,0:T(8,128)(2,1)} %bitcast.73), kind=kOutput, calls=%fused_computation.12 | convolution fusion | flops 234881024 | bytes 4587520 | tf_op jit(solution)/shard_map/trm,rim->tri/dot_general | solution.py:29
  32.4 0.0 copy-done.1
  32.4 1.6 convolution_bitcast_fusion.3
  34.1 4.1 %copy.81 = bf16[128,8192]{0,1:T(8,128)(2,1)} copy(bf16[128,8192]{1,0:T(8,128)(2,1)} %param.10) | data formatting | bytes 4194304 | tf_op args[1]
  38.2 4.1 %copy.82 = bf16[128,64,128]{2,0,1:T(8,128)(2,1)} copy(bf16[128,64,128]{0,2,1:T(8,128)(2,1)} %bitcast.72) | data formatting | bytes 4194304 | tf_op jit(solution)/shard_map/reshape | solution.py:39
  42.3 3.6 %gather_fusion.1 = bf16[56,128,128]{2,1,0:T(8,128)(2,1)} fusion(bf16[128,64,128]{2,0,1:T(8,128)(2,1)} %copy.82, s32[1024]{0:T(1024)S(1)} %pad_clamp_fusion), kind=kCustom, calls=%fused_computation.1.clone | custom fusion | bytes 3670240 | tf_op jit(solution)/shard_map/jit(_take)/gather | solution.py:39
  45.9 3.0 %select_bitcast_fusion = bf16[128,56,128]{2,0,1:T(8,128)(2,1)} fusion(bf16[56,128,128]{2,1,0:T(8,128)(2,1)} %gather_fusion.1, pred[56]{0:T(512)(128)(4,1)S(1)} %get-tuple-element.28), kind=kLoop, calls=%fused_computation.6 | loop fusion | flops 917504 | bytes 3670072 | tf_op jit(solution)/shard_map/jit(_take)/select_n | solution.py:39
  48.8 3.9 %copy.83 = bf16[128,56,128]{0,2,1:T(8,128)(2,1)} copy(bf16[128,56,128]{2,0,1:T(8,128)(2,1)} %select_bitcast_fusion) | data formatting | bytes 3670016 | tf_op jit(solution)/shard_map/jit(_take)/select_n | solution.py:39
  52.7 0.0 copy-done
  52.7 3.1 %multiply_convert_fusion = (bf16[128,14,128]{2,0,1:T(8,128)(2,1)S(1)}, bf16[128,14,128]{2,0,1:T(8,128)(2,1)S(1)}, bf16[128,14,128]{2,0,1:T(8,128)(2,1)S(1)}) fusion(f32[128,14,128]{2,0,1:T(8,128)} %convolution_bitcast_fusion.3, f32[128,14,128]{2,0,1:T(8,128)} %convolution_bitcast_fusion.2, bf16[128,14,512]{0,2,1:T(8,128)(2,1)} %bitcast.77, ...), kind=kOutput, calls=%fused_computation.14 | convolution fusion | flops 238321664 | bytes 6881280 | tf_op jit(solution)/shard_map/trm,rim->tri/dot_general | solution.py:42
  55.8 0.7 convolution_convert_fusion.1
  56.5 0.2 pad.2
  56.8 2.5 copy.105
  59.3 0.7 convolution_convert_fusion
  60.0 0.2 pad.3
  60.2 2.5 copy.106
  62.7 0.0 all-reduce.3.cloned.1.call-update
  62.7 0.2 reduce-scatter.5.cloned.1.call-start
  63.0 0.1 reshape.128
  63.1 0.1 reshape.136
  63.2 0.0 copy-start.3
  63.2 2.3 fusion.3
  65.4 0.0 copy-done.3
  65.4 2.5 add_bitcast_fusion
  67.9 5.1 %copy.85 = f32[128,14,512]{0,2,1:T(8,128)} copy(f32[128,14,512]{2,0,1:T(8,128)} %add_bitcast_fusion) | data formatting | bytes 7340032 | tf_op jit(solution)/shard_map/add | solution.py:65
  73.0 5.4 %copy.86 = f32[56,128,128]{2,1,0:T(8,128)} copy(f32[56,128,128]{1,2,0:T(8,128)} %bitcast.63) | data formatting | bytes 7340032 | tf_op jit(solution)/shard_map/reshape | solution.py:66
  78.4 2.5 broadcast.43.clone.1
  80.8 13.4 %scatter_fusion.1 = f32[128,64,128]{2,0,1:T(8,128)} fusion(f32[128,64,128]{2,0,1:T(8,128)} %broadcast.43.clone.1, s32[56]{0:T(128)S(1)} %get-tuple-element.31, f32[56,128,128]{2,1,0:T(8,128)} %copy.86), kind=kCustom, calls=%fused_computation.3 | custom fusion | flops 917504 | bytes 11010272 | tf_op jit(solution)/shard_map/scatter-add | solution.py:13
  94.3 4.0 %convert_element_type.66 = bf16[128,64,128]{2,0,1:T(8,128)(2,1)} convert(f32[128,64,128]{2,0,1:T(8,128)} %scatter_fusion.1) | non-fusion elementwise | flops 1048576 | bytes 6291456 | tf_op jit(solution)/shard_map/convert_element_type | solution.py:67
  98.2 4.1 %copy.87 = bf16[128,64,128]{0,2,1:T(8,128)(2,1)} copy(bf16[128,64,128]{2,0,1:T(8,128)(2,1)} %convert_element_type.66) | data formatting | bytes 4194304 | tf_op jit(solution)/shard_map/convert_element_type | solution.py:67
  102.3 0.0 reduce-scatter.5.cloned.1.call-update
  102.3 0.0 reduce-scatter.3.cloned.1.call-start
  102.4 2.5 convolution_bitcast_fusion
  104.8 5.1 %copy.76 = f32[128,14,512]{0,2,1:T(8,128)} copy(f32[128,14,512]{2,0,1:T(8,128)} %convolution_bitcast_fusion) | data formatting | bytes 7340032 | tf_op jit(solution)/shard_map/tri,rim->trm/transpose | solution.py:33
  109.9 5.4 %copy.77 = f32[56,128,128]{2,1,0:T(8,128)} copy(f32[56,128,128]{1,2,0:T(8,128)} %bitcast.64) | data formatting | bytes 7340032 | tf_op jit(solution)/shard_map/reshape | solution.py:34
  115.3 2.5 broadcast.43.clone
  117.8 13.5 %scatter_fusion = f32[128,64,128]{2,0,1:T(8,128)} fusion(f32[128,64,128]{2,0,1:T(8,128)} %broadcast.43.clone, s32[56]{0:T(128)S(1)} %get-tuple-element.30, f32[56,128,128]{2,1,0:T(8,128)} %copy.77), kind=kCustom, calls=%fused_computation.2 | custom fusion | flops 917504 | bytes 11010272 | tf_op jit(solution)/shard_map/scatter-add | solution.py:13
  131.3 4.0 %convert_element_type.62 = bf16[128,64,128]{2,0,1:T(8,128)(2,1)} convert(f32[128,64,128]{2,0,1:T(8,128)} %scatter_fusion) | non-fusion elementwise | flops 1048576 | bytes 6291456 | tf_op jit(solution)/shard_map/convert_element_type | solution.py:35
  135.3 4.2 %copy.78 = bf16[128,64,128]{0,2,1:T(8,128)(2,1)} copy(bf16[128,64,128]{2,0,1:T(8,128)(2,1)} %convert_element_type.62) | data formatting | bytes 4194304 | tf_op jit(solution)/shard_map/convert_element_type | solution.py:35
  139.4 0.0 reduce-scatter.3.cloned.1.call-update
  139.4 0.0 all-gather.2.cloned.1.call-start
  139.5 3.4 %convolution_convert_fusion.2 = bf16[14,128,512]{2,1,0:T(8,128)(2,1)} fusion(bf16[128,14,128]{2,0,1:T(8,128)(2,1)S(1)} %get-tuple-element.24, bf16[128,14,512]{0,2,1:T(8,128)(2,1)} %bitcast.60), kind=kOutput, calls=%fused_computation.10 | convolution fusion | flops 235798528 | bytes 4128768 | tf_op jit(solution)/shard_map/tri,trm->rim/dot_general | solution.py:48
  142.9 3.2 %convert_element_type.69 = bf16[1,14,65536]{2,1,0:T(8,128)(2,1)} reshape(bf16[14,128,512]{2,1,0:T(8,128)(2,1)} %convolution_convert_fusion.2) | data formatting | bytes 3670016 | tf_op jit(solution)/shard_map/convert_element_type | solution.py:55
  146.1 0.0 all-gather.2.cloned.1.call-update
  146.1 0.0 all-reduce.3.cloned.1.call-done
  146.2 1.8 dynamic-slice_convert_fusion
  148.0 1.8 dynamic-slice_convert_fusion.1
  149.7 29.2 %reduce-scatter.5.cloned.1.call-done = bf16[128,512]{0,1:T(8,128)(2,1)} async-done(((bf16[128,8192]{0,1:T(8,128)(2,1)}), bf16[128,512]{0,1:T(8,128)(2,1)}) %reduce-scatter.5.cloned.1.call-update) | async-done | bytes 131088 | tf_op jit(solution)/shard_map/reduce_scatter | solution.py:68
  179.0 1.7 copy.95
  180.6 75.5 %reduce-scatter.3.cloned.1.call-done = bf16[128,512]{0,1:T(8,128)(2,1)} async-done(((bf16[128,8192]{0,1:T(8,128)(2,1)}), bf16[128,512]{0,1:T(8,128)(2,1)}) %reduce-scatter.3.cloned.1.call-update) | async-done | bytes 131088 | tf_op jit(solution)/shard_map/reduce_scatter | solution.py:36
  256.2 1.7 copy.94
  257.8 11.0 %reduce_sum.12 = bf16[14,65536]{1,0:T(8,128)(2,1)} reduce(bf16[8,14,65536]{2,1,0:T(8,128)(2,1)} %all-gather.2.cloned.1.call-done, bf16[]{:T(256)} %constant.11.clone.1), dimensions={0}, to_apply=%region_4.6 | reduce | flops 6422528 | bytes 16515074 | tf_op jit(solution)/shard_map/reduce_sum | solution.py:55
  268.9 1.8 dynamic-slice_convert_fusion.2
  (13 shorter events, 0.0 us)
Async XLA Ops:
  8.0 44.7 %copy-start = (bf16[1792,512]{1,0:T(8,128)(2,1)S(1)}, bf16[1792,512]{1,0:T(8,128)(2,1)}, u32[]{:S(2)}) copy-start(bf16[1792,512]{1,0:T(8,128)(2,1)} %param.13) | copy-start | bytes 5505028
  8.0 138.1 %all-reduce.3.cloned.1.call-start = ((), (), s32[]{:S(2)}) async-start(), calls=%async_computation.5 | async-start | bytes 8388608 | tf_op jit(solution)/shard_map/psum | solution.py:56
  28.6 3.9 %copy-start.1 = (bf16[128,56,128]{0,2,1:T(8,128)(2,1)S(1)}, bf16[128,56,128]{0,2,1:T(8,128)(2,1)}, u32[]{:S(2)}) copy-start(bf16[128,56,128]{0,2,1:T(8,128)(2,1)} %copy.73) | copy-start | bytes 5505028
  28.6 3.9 %copy-start.4 = (bf16[1792,512]{1,0:T(8,128)(2,1)S(1)}, bf16[1792,512]{1,0:T(8,128)(2,1)}, u32[]{:S(2)}) copy-start(bf16[1792,512]{1,0:T(8,128)(2,1)} %param.11) | copy-start | bytes 5505028
  52.7 3.1 %copy-start.2 = (bf16[128,56,128]{0,2,1:T(8,128)(2,1)S(1)}, bf16[128,56,128]{0,2,1:T(8,128)(2,1)}, u32[]{:S(2)}) copy-start(bf16[128,56,128]{0,2,1:T(8,128)(2,1)} %copy.73) | copy-start | bytes 5505028
  56.7 2.5 copy-start.5
  62.7 116.2 %reduce-scatter.5.cloned.1.call-start = ((), (), s32[]{:S(2)}) async-start(), calls=%async_computation.3 | async-start | bytes 2228224 | tf_op jit(solution)/shard_map/reduce_scatter | solution.py:68
  63.2 2.3 copy-start.3
  102.3 153.8 %reduce-scatter.3.cloned.1.call-start = ((), (), s32[]{:S(2)}) async-start(), calls=%async_computation.2 | async-start | bytes 2228224 | tf_op jit(solution)/shard_map/reduce_scatter | solution.py:36
  139.4 118.4 %all-gather.2.cloned.1.call-start = ((), (), s32[]{:S(2)}) async-start(), calls=%async_computation.4 | async-start | bytes 18874368 | tf_op jit(solution)/shard_map/all_gather | solution.py:55
Sparse Core Ops, SparseCore 0:
  62.9 75.9 all-reduce.2
  146.2 87.2 all-gather.1
Sparse Core Ops, SparseCore 1:
  102.4 76.5 reduce-scatter.4
  182.4 73.7 reduce-scatter.2
